TPU v7x, 32 devices: a whole 2x2x4 slice. The times are simulated.
32 devices in a mesh: dp: 8 (over y, x, core), tensor: 4 (over z).
Axes of the slice: x: 2, y: 2, z: 4, core: 2. Of those that a mesh axis runs over, the one named last changes fastest.
Arguments:
- tokens: bfloat16 [16384, 768], P(('dp', 'tensor')), may hold values from -6 to 6
- cotangent: bfloat16 [16384, 768], P(('dp', 'tensor')), may hold values from -6 to 6, as said below
- segment: int32 [32, 512], P(('dp', 'tensor')), may hold values from 0 to 11, never falling along the last dimension, each value on 1 to 202 neighbouring positions
- projection: float32 [64, 32], replicated, may hold values from -5 to 5
- first_gain: float32 [768], replicated, may hold values from 0.5 to 1.5
- first_bias: float32 [768], replicated, may hold values from -4 to 4
- w_query: bfloat16 [768, 768], replicated, may hold values from -0.109375 to 0.109375
- w_key: bfloat16 [768, 768], replicated, may hold values from -0.109375 to 0.109375
- w_value: bfloat16 [768, 768], replicated, may hold values from -0.21875 to 0.21875
- w_out: bfloat16 [768, 768], replicated, may hold values from -1.25 to 1.25
- b_query: float32 [768], replicated, may hold values from -4 to 4
- b_key: float32 [768], replicated, may hold values from -4 to 4
- b_value: float32 [768], replicated, may hold values from -4 to 4
- b_out: float32 [768], replicated, may hold values from -4 to 4
- second_gain: float32 [768], replicated, may hold values from 0.5 to 1.5
- second_bias: float32 [768], replicated, may hold values from -4 to 4
- w_up: bfloat16 [768, 3072], P(None, 'tensor'), may hold values from -0.21875 to 0.21875
- b_up: float32 [3072], P('tensor'), may hold values from -4 to 4
- w_down: bfloat16 [3072, 768], P('tensor'), may hold values from -0.109375 to 0.109375
- b_down: float32 [768], replicated, may hold values from -4 to 4
Outputs:
- output: bfloat16 [16384, 768], P(('dp', 'tensor'))
- grad_tokens: bfloat16 [16384, 768], P(('dp', 'tensor'))
- grad_first_gain: float32 [768], replicated
- grad_first_bias: float32 [768], replicated
- grad_w_query: float32 [768, 768], replicated
- grad_w_key: float32 [768, 768], replicated
- grad_w_value: float32 [768, 768], replicated
- grad_w_out: float32 [768, 768], replicated
- grad_b_query: float32 [768], replicated
- grad_b_key: float32 [768], replicated
- grad_b_value: float32 [768], replicated
- grad_b_out: float32 [768], replicated
- grad_second_gain: float32 [768], replicated
- grad_second_bias: float32 [768], replicated
- grad_w_up: float32 [768, 3072], P(None, 'tensor')
- grad_b_up: float32 [3072], P('tensor')
- grad_w_down: float32 [3072, 768], P('tensor')
- grad_b_down: float32 [768], replicated
Inputs may be any that keep to these rules, and one draw needn't show every extreme that they name: `segment`: within each row of 512 tokens, molecule numbers never fall; each molecule has 1 to 202 tokens and one has exactly 202. `cotangent`: gradient rows of order one.
All inputs are finite; a program needn't handle non-finite values.
Results may differ from a plain program's by a relative error of at most 0.01.
Values may be sent and summed in bfloat16 or wider, within the bound.
No kernel may reach another device: no remote copies, remote signals or barrier semaphores. Data moves between devices by JAX's collectives and lax.ppermute only.
A program may use at most 192 MiB of HBM per device.

v0:
```python
from functools import partial
import math
import jax
import jax.numpy as jnp
from jax import lax
from jax.sharding import PartitionSpec as P

HEADS = 12
highest_precision = lax.Precision.HIGHEST


def layer_norm(inputs, gain, shift):
    average = jnp.mean(inputs, -1, keepdims=True)
    centred = inputs - average
    spread = jnp.mean(centred * centred, -1, keepdims=True)
    return centred * lax.rsqrt(spread + 1e-05) * gain + shift


def positions(labels):
    places = jnp.arange(labels.shape[0], dtype=jnp.int32)
    matches = labels[:, None] == labels[None, :]
    before = places[None, :] < places[:, None]
    return jnp.sum((matches & before).astype(jnp.int32), axis=1)


def rotate(inputs, places):
    split_at = inputs.shape[-1] // 2
    ladder = jnp.arange(split_at).astype(jnp.float32)
    speeds = jnp.exp(ladder * (-2.0 * math.log(10000.0) / inputs.shape[-1]))
    angles = places.astype(jnp.float32)[:, None] * speeds[None, :]
    cosine = jnp.cos(angles)[:, None, :]
    sine_part = jnp.sin(angles)[:, None, :]
    lower_half = inputs[..., :split_at]
    upper_half = inputs[..., split_at:]
    return jnp.concatenate(
        [
            lower_half * cosine - upper_half * sine_part,
            upper_half * cosine + lower_half * sine_part,
        ],
        -1,
    )


def features(inputs, projection):
    scaled = inputs * inputs.shape[-1] ** (-0.25)
    projected = jnp.einsum("rhd,df->rhf", scaled, projection, precision=highest_precision)
    return jnp.exp(
        projected - 0.5 * jnp.sum(scaled * scaled, -1, keepdims=True)
    ) * projection.shape[-1] ** (-0.5)


def attend(queries, key_rows, value_rows, labels, projection):
    row_count = queries.shape[0]
    places = positions(labels)
    query_feature_map = features(rotate(queries.reshape(row_count, HEADS, -1), places), projection)
    key_feature_map = features(rotate(key_rows.reshape(row_count, HEADS, -1), places), projection)
    value_heads = value_rows.reshape(row_count, HEADS, -1)
    attention_scores = jnp.einsum(
        "otg,atg->toa", query_feature_map, key_feature_map, precision=highest_precision
    )
    matches = (labels[:, None] == labels[None, :]).astype(attention_scores.dtype)
    weights = attention_scores * matches[None]
    totals = jnp.sum(weights, -1)
    mixture = jnp.einsum("hqk,khd->qhd", weights, value_heads, precision=highest_precision)
    return (mixture / jnp.transpose(totals)[:, :, None]).reshape(row_count, -1)


def matmul(left, right):
    return jnp.dot(left, right, preferred_element_type=jnp.float32)


def left_product(left, right):
    return lax.dot_general(
        left, right, (((0,), (0,)), ((), ())), preferred_element_type=jnp.float32
    )


def right_product(left, right):
    return lax.dot_general(
        left, right, (((1,), (1,)), ((), ())), preferred_element_type=jnp.float32
    )


def column_sum(values):
    return jnp.sum(values.astype(jnp.float32), 0)


def body(
    tokens,
    cotangent,
    segment,
    projection,
    first_gain,
    first_bias,
    w_query,
    w_key,
    w_value,
    w_out,
    b_query,
    b_key,
    b_value,
    b_out,
    second_gain,
    second_bias,
    w_up,
    b_up,
    w_down,
    b_down,
):
    row_count = tokens.shape[0]
    labels = segment[0]
    widened = tokens.astype(jnp.float32)
    normed, first_back = jax.vjp(layer_norm, widened, first_gain, first_bias)
    normed_low = normed.astype(jnp.bfloat16)
    queries = matmul(normed_low, w_query) + b_query
    key_rows = matmul(normed_low, w_key) + b_key
    value_rows = matmul(normed_low, w_value) + b_value

    def attend_here(query_in, key_in, value_in):
        return attend(query_in, key_in, value_in, labels, projection)

    context, kernel_core_pullback = jax.vjp(attend_here, queries, key_rows, value_rows)
    context_low = context.astype(jnp.bfloat16)
    middle = widened + matmul(context_low, w_out) + b_out
    second, second_back = jax.vjp(layer_norm, middle, second_gain, second_bias)
    second_low = second.astype(jnp.bfloat16)
    upstream = cotangent.astype(jnp.float32)
    down_bias_grad = jnp.sum(upstream, 0)
    gathered = lax.all_gather(second_low, "tensor", axis=0, tiled=True)
    inner_rows = matmul(gathered, w_up) + b_up
    hidden, gelu_back = jax.vjp(partial(jax.nn.gelu, approximate=False), inner_rows)
    hidden_low = hidden.astype(jnp.bfloat16)
    branch = lax.psum_scatter(
        matmul(
            lax.slice_in_dim(hidden_low, 0, row_count * lax.axis_size("tensor"), axis=0), w_down
        ).astype(jnp.bfloat16),
        "tensor",
        scatter_dimension=0,
        tiled=True,
    ).astype(jnp.float32)
    output = (middle + branch + b_down).astype(jnp.bfloat16)
    cot_gathered = lax.all_gather(cotangent, "tensor", axis=0, tiled=True)
    down_grad = left_product(hidden_low, cot_gathered)
    hidden_grad = right_product(cot_gathered, w_down)
    inner_grad = gelu_back(hidden_grad)[0].astype(jnp.bfloat16)
    up_bias_grad = column_sum(inner_grad)
    up_grad = left_product(gathered, inner_grad)
    second_grad = lax.psum_scatter(
        right_product(inner_grad, w_up).astype(jnp.bfloat16),
        "tensor",
        scatter_dimension=0,
        tiled=True,
    ).astype(jnp.float32)
    up_grad, up_bias_grad, down_grad = lax.psum((up_grad, up_bias_grad, down_grad), "dp")
    middle_back, gain_two_grad, bias_two_grad = second_back(second_grad)
    middle_grad = upstream + middle_back
    out_grad_low = middle_grad.astype(jnp.bfloat16)
    wout_grad = left_product(context_low, out_grad_low)
    bout_grad = column_sum(out_grad_low)
    context_grad = right_product(out_grad_low, w_out)
    query_grad, key_grad, value_grad = kernel_core_pullback(context_grad)
    query_low = query_grad.astype(jnp.bfloat16)
    key_low = key_grad.astype(jnp.bfloat16)
    value_low = value_grad.astype(jnp.bfloat16)
    query_weight_grad = left_product(normed_low, query_low)
    wkey_grad = left_product(normed_low, key_low)
    value_weight_grad = left_product(normed_low, value_low)
    bquery_grad = column_sum(query_low)
    bkey_grad = column_sum(key_low)
    bvalue_grad = column_sum(value_low)
    normed_grad = (
        right_product(query_low, w_query)
        + right_product(key_low, w_key)
        + right_product(value_low, w_value)
    )
    token_back, gain_one_grad, bias_one_grad = first_back(normed_grad)
    grad_tokens = (middle_grad + token_back).astype(jnp.bfloat16)
    (
        gain_one_grad,
        bias_one_grad,
        query_weight_grad,
        wkey_grad,
        value_weight_grad,
        wout_grad,
        bquery_grad,
        bkey_grad,
        bvalue_grad,
        bout_grad,
        gain_two_grad,
        bias_two_grad,
        down_bias_grad,
    ) = lax.psum(
        (
            gain_one_grad,
            bias_one_grad,
            query_weight_grad,
            wkey_grad,
            value_weight_grad,
            wout_grad,
            bquery_grad,
            bkey_grad,
            bvalue_grad,
            bout_grad,
            gain_two_grad,
            bias_two_grad,
            down_bias_grad,
        ),
        ("dp", "tensor"),
    )
    return (
        output,
        grad_tokens,
        gain_one_grad,
        bias_one_grad,
        query_weight_grad,
        wkey_grad,
        value_weight_grad,
        wout_grad,
        bquery_grad,
        bkey_grad,
        bvalue_grad,
        bout_grad,
        gain_two_grad,
        bias_two_grad,
        up_grad,
        up_bias_grad,
        down_grad,
        down_bias_grad,
    )


def solution(mesh):
    return jax.shard_map(
        body,
        mesh=mesh,
        in_specs=(
            P(("dp", "tensor"), None),
            P(("dp", "tensor"), None),
            P(("dp", "tensor"), None),
            P(),
            P(),
            P(),
            P(),
            P(),
            P(),
            P(),
            P(),
            P(),
            P(),
            P(),
            P(),
            P(),
            P(None, "tensor"),
            P("tensor"),
            P("tensor", None),
            P(),
        ),
        out_specs=(
            P(("dp", "tensor"), None),
            P(("dp", "tensor"), None),
            P(),
            P(),
            P(),
            P(),
            P(),
            P(),
            P(),
            P(),
            P(),
            P(),
            P(),
            P(),
            P(None, "tensor"),
            P("tensor"),
            P("tensor", None),
            P(),
        ),
        check_vma=False,
    )
```

profile of v0, /device:TPU:0, one launch (start us, length us, event | category | flops | bytes accessed | tf_op | source)
XLA Modules:
  0.0 651.4 jit_solution(13527128081990880448)
XLA Ops:
  9.8 2.1 convolution_add_fusion.1
  11.9 3.0 copy.50
  14.9 3.3 convolution_add_fusion
  18.3 3.0 copy.51
  21.6 2.3 multiply_subtract_fusion.1
  25.1 2.0 fusion.53
  27.1 2.0 fusion.59
  29.0 2.1 convolution_add_fusion.2
  31.1 3.0 copy.49
  34.1 12.6 %multiply_reduce_fusion = (f32[12,512]{1,0:T(8,128)S(1)}, f32[12,512,512]{1,2,0:T(8,128)S(1)}) fusion(f32[512,512]{0,1:T(8,128)S(1)} %compare_convert_fusion, f32[512,12,32]{0,2,1:T(8,128)} %fusion.59, f32[512,12,32]{0,2,1:T(8,128)} %fusion.53), kind=kOutput, calls=%fused_computation.5 | convolution fusion | flops 1214638080 | bytes 15228928 | tf_op jit(solution)/shard_map/jvp(otg,atg->toa)/dot_general | solution.py:58
  46.7 9.7 %fusion.37 = (bf16[512,12,64]{0,2,1:T(8,128)(2,1)S(1)}, f32[12,64,512]{2,1,0:T(8,128)}) fusion(f32[512,12]{0,1:T(8,128)S(1)} %bitcast.95, f32[512,12,64]{0,2,1:T(8,128)S(1)} %bitcast.84, f32[12,512,512]{1,2,0:T(8,128)S(1)} %get-tuple-element.69, f32[512,512]{0,1:T(8,128)S(1)} %compare_convert_fusion), kind=kOutput, calls=%fused_computation.67 | convolution fusion | flops 2419851264 | bytes 17588224 | tf_op jit(solution)/shard_map/jvp(hqk,khd->qhd)/dot_general | solution.py:64
  60.5 65.5 %all-gather.3.cloned.1.call-done = bf16[2048,768]{1,0:T(8,128)(2,1)} async-done(((bf16[512,768]{1,0:T(8,128)(2,1)}), bf16[2048,768]{1,0:T(8,128)(2,1)}) %all-gather.3.cloned.1.call-update) | async-done | bytes 3145744 | tf_op jit(solution)/shard_map/all_gather | solution.py:129
  126.1 7.4 %fusion.109 = f32[2048,768]{1,0:T(8,128)} fusion(bf16[2048,768]{1,0:T(8,128)(2,1)} %all-gather.3.cloned.1.call-done, bf16[768,768]{1,0:T(8,128)(2,1)} %param.36), kind=kOutput, calls=%fused_computation.167 | convolution fusion | flops 2415919104 | bytes 10616832 | tf_op jit(solution)/shard_map/dot_general | solution.py:69
  133.5 56.3 %all-gather.5.cloned.1.call-done = bf16[2048,768]{1,0:T(8,128)(2,1)} async-done(((bf16[512,768]{1,0:T(8,128)(2,1)}), bf16[2048,768]{1,0:T(8,128)(2,1)}) %all-gather.5.cloned.1.call-update) | async-done | bytes 3145744 | tf_op jit(solution)/shard_map/all_gather | solution.py:142
  189.8 19.6 %convert_reduce_fusion = (f32[768]{0:T(1024)S(1)}, bf16[2048,768]{1,0:T(8,128)(2,1)S(1)}, f32[2048,768]{1,0:T(8,128)}) fusion(f32[2048,768]{1,0:T(8,128)} %fusion.109, f32[768]{0:T(1024)S(1)} %copy-done.41, bf16[2048,768]{1,0:T(8,128)(2,1)} %all-gather.5.cloned.1.call-done, bf16[768,768]{1,0:T(8,128)(2,1)S(1)} %copy-done), kind=kOutput, calls=%fused_computation.10 | convolution fusion | flops 2533883136 | bytes 20060160 | tf_op jit(solution)/shard_map/dot_general | solution.py:79
  209.4 1.7 copy-done.54
  211.2 4.0 convolution_convert_fusion
  215.3 5.5 multiply_convert_fusion
  220.8 1.6 copy-done.24
  222.4 3.9 convolution_convert_fusion.1
  226.5 7.1 %fusion.114 = f32[768,768]{1,0:T(8,128)} fusion(bf16[2048,768]{1,0:T(8,128)(2,1)} %all-gather.3.cloned.1.call-done, bf16[2048,768]{1,0:T(8,128)(2,1)} %copy-done.54), kind=kOutput, calls=%fused_computation.172 | convolution fusion | flops 2415919104 | bytes 8650752 | tf_op jit(solution)/shard_map/dot_general | solution.py:73
  233.6 4.2 fusion.115
  238.3 36.0 %reduce-scatter.5.cloned.1.call-done = bf16[512,768]{1,0:T(8,128)(2,1)} async-done(((bf16[2048,768]{1,0:T(8,128)(2,1)}), bf16[512,768]{1,0:T(8,128)(2,1)}) %reduce-scatter.5.cloned.1.call-update) | async-done | bytes 786448 | tf_op jit(solution)/shard_map/reduce_scatter | solution.py:148
  274.3 2.3 fusion.33
  276.6 60.1 %reduce-scatter.3.cloned.1.call-done = bf16[512,768]{1,0:T(8,128)(2,1)} async-done(((bf16[2048,768]{1,0:T(8,128)(2,1)}), bf16[512,768]{1,0:T(8,128)(2,1)}) %reduce-scatter.3.cloned.1.call-update) | async-done | bytes 786448 | tf_op jit(solution)/shard_map/reduce_scatter | solution.py:133
  336.7 3.5 fusion.105
  343.5 10.5 %fusion.35 = f32[12,512,512]{1,2,0:T(8,128)S(1)} fusion(f32[512,12,64]{0,2,1:T(8,128)S(1)} %bitcast.85, f32[512,12,64]{0,2,1:T(8,128)S(1)} %bitcast.86, f32[512,12]{0,1:T(8,128)S(1)} %bitcast.96), kind=kOutput, calls=%fused_computation.63 | convolution fusion | flops 2416312320 | bytes 15753216 | tf_op jit(solution)/shard_map/transpose(jvp(hqk,khd->qhd))/dot_general | solution.py:64
  355.4 8.6 %fusion.108 = (f32[512,12]{0,1:T(8,128)S(1)}, f32[512,12,32]{0,2,1:T(8,128)S(1)}) fusion(f32[512,12,32]{0,2,1:T(8,128)S(1)} %copy-done.9, f32[512,12,32]{0,2,1:T(8,128)S(1)} %copy-done.10, f32[12,512,512]{1,2,0:T(8,128)S(1)} %fusion.35, f32[12,512]{1,0:T(8,128)S(1)} %negate_bitcast_fusion, f32[512,512]{0,1:T(8,128)S(1)} %compare_convert_fusion), kind=kOutput, calls=%fused_computation.166 | convolution fusion | flops 1215031296 | bytes 16039936 | tf_op jit(solution)/shard_map/transpose(jvp(otg,atg->toa))/dot_general | solution.py:58
  364.1 12.9 %fusion.107 = (f32[512,12]{0,1:T(8,128)S(1)}, f32[512,12,32]{0,2,1:T(8,128)S(1)}) fusion(f32[512,12,32]{0,2,1:T(8,128)S(1)} %copy-done.10, f32[512,12,32]{0,2,1:T(8,128)S(1)} %copy-done.9, f32[12,512,512]{1,2,0:T(8,128)S(1)} %fusion.35, f32[12,512]{1,0:T(8,128)S(1)} %negate_bitcast_fusion, f32[512,512]{0,1:T(8,128)S(1)} %compare_convert_fusion), kind=kOutput, calls=%fused_computation.165 | convolution fusion | flops 1215031296 | bytes 16039936 | tf_op jit(solution)/shard_map/transpose(jvp(otg,atg->toa))/dot_general | solution.py:58
  377.1 1.7 fusion.40
  378.8 1.7 fusion.39
  381.6 1.3 copy-done.23
  383.0 2.2 fusion.113
  385.2 2.9 fusion.95
  388.1 2.5 fusion.97
  390.6 12.1 %convert_reduce_fusion.5 = (f32[12,64]{1,0:T(8,128)S(1)}, bf16[12,64,512]{2,1,0:T(8,128)(2,1)S(1)}) fusion(f32[12,512,512]{1,2,0:T(8,128)S(1)} %bitcast.83, f32[512,512]{0,1:T(8,128)S(1)} %compare_convert_fusion, f32[512,12,64]{0,2,1:T(8,128)S(1)} %bitcast.88, f32[512,12]{0,1:T(8,128)S(1)} %bitcast.97), kind=kOutput, calls=%fused_computation.74 | convolution fusion | flops 2420636928 | bytes 16018432 | tf_op jit(solution)/shard_map/transpose(jvp(hqk,khd->qhd))/dot_general | solution.py:64
  402.7 2.5 fusion.93
  405.2 14.8 %psum.125 = f32[768]{0:T(1024)} all-reduce(f32[768]{0:T(1024)S(1)} %get-tuple-element.40), channel_id=1, replica_groups=mesh['dp'=8,'tensor'=4] {'dp'}, use_global_device_ids=true, to_apply=%region_39.0 | all-reduce | flops 768 | bytes 6144 | tf_op jit(solution)/shard_map/psum | solution.py:154
  420.2 2.3 fusion.112
  426.6 1.7 convert_reduce_fusion.3
  428.3 42.2 %all-reduce.4 = (f32[768]{0:T(1024)}, f32[768]{0:T(1024)}, f32[768]{0:T(1024)}, f32[768]{0:T(1024)}, f32[768]{0:T(1024)}, /*index=5*/f32[768]{0:T(1024)}, f32[768]{0:T(1024)}, f32[768]{0:T(1024)}, f32[768]{0:T(1024)}) all-reduce(f32[768]{0:T(1024)S(1)} %get-tuple-element.18, ...), channel_id=1, replica_groups=mesh['dp'=8,'tensor'=4] {'dp','tensor'}, use_global_device_ids=true, to_apply=%region_18.0 | all-reduce | flops 6912 | bytes 55296 | tf_op jit(solution)/shard_map/psum | solution.py:192
  470.5 159.0 %all-reduce.10.cloned.1.call-done = (f32[768,768]{1,0:T(8,128)}, f32[768,768]{1,0:T(8,128)}, f32[768,768]{1,0:T(8,128)}, f32[768,768]{1,0:T(8,128)}) async-done(((f32[768,768]{1,0:T(8,128)}, f32[768,768]{1,0:T(8,128)}, f32[768,768]{1,0:T(8,128)}, f32[768,768]{1,0:T(8,128)}), (f32[768,768]{1,0:T(8,128)}, f32[768,768]{1,0:T(8,128)}, f32[768,768]{1,0:T(8,128)}, ...) | async-done | bytes 9437200 | tf_op jit(solution)/shard_map/psum | solution.py:192
  629.5 3.4 copy.70
  632.9 1.4 copy.71
  635.4 1.4 copy.72
  638.0 1.4 copy.73
  640.5 1.4 copy.74
  643.0 1.4 copy.75
  (164 shorter events, 23.2 us)
Async XLA Ops:
  7.2 182.7 %copy-start = (bf16[768,768]{1,0:T(8,128)(2,1)S(1)}, bf16[768,768]{1,0:T(8,128)(2,1)}, u32[]{:S(2)}) copy-start(bf16[768,768]{1,0:T(8,128)(2,1)} %param.38) | copy-start | bytes 3538948
  7.2 2.0 copy-start.4
  7.2 2.6 copy-start.38
  7.2 2.6 copy-start.53
  7.2 2.6 copy-start.49
  7.2 118.8 %all-gather.3.cloned.1.call-start = ((), (), s32[]{:S(2)}) async-start(), calls=%async_computation.2 | async-start | bytes 3932160 | tf_op jit(solution)/shard_map/all_gather | solution.py:129
  7.3 2.5 copy-start.47
  11.9 3.0 copy-start.50
  24.0 3.1 copy-start.11
  24.0 3.1 copy-start.13
  27.1 2.0 copy-start.31
  27.1 2.0 copy-start.51
  34.1 12.6 %copy-start.7 = (f32[512,768]{0,1:T(8,128)S(1)}, f32[512,768]{0,1:T(8,128)}, u32[]{:S(2)}) copy-start(f32[512,768]{0,1:T(8,128)} %copy.49) | copy-start | bytes 4718596
  46.7 9.7 %copy-start.2 = (f32[12,512,512]{1,2,0:T(8,128)}, f32[12,512,512]{1,2,0:T(8,128)S(1)}, u32[]{:S(2)}) copy-start(f32[12,512,512]{1,2,0:T(8,128)S(1)} %get-tuple-element.69) | copy-start | bytes 37748740
  46.7 9.7 %copy-start.45 = (bf16[768,768]{1,0:T(8,128)(2,1)S(1)}, bf16[768,768]{1,0:T(8,128)(2,1)}, u32[]{:S(2)}) copy-start(bf16[768,768]{1,0:T(8,128)(2,1)} %param.29) | copy-start | bytes 3538948
  46.7 9.7 %copy-start.52 = (f32[768]{0:T(1024)S(1)}, f32[768]{0:T(1024)}, u32[]{:S(2)}) copy-start(f32[768]{0:T(1024)} %param.33) | copy-start | bytes 9220
  59.7 130.1 %all-gather.5.cloned.1.call-start = ((), (), s32[]{:S(2)}) async-start(), calls=%async_computation.4 | async-start | bytes 3932160 | tf_op jit(solution)/shard_map/all_gather | solution.py:142
  60.5 129.4 %copy-start.41 = (f32[768]{0:T(1024)S(1)}, f32[768]{0:T(1024)}, u32[]{:S(2)}) copy-start(f32[768]{0:T(1024)} %param.37) | copy-start | bytes 9220
  60.5 213.8 %reduce-scatter.5.cloned.1.call-start = ((), (), s32[]{:S(2)}) async-start(), calls=%async_computation.5 | async-start | bytes 3932160 | tf_op jit(solution)/shard_map/reduce_scatter | solution.py:148
  189.8 21.3 %copy-start.44 = (bf16[768,768]{1,0:T(8,128)(2,1)S(1)}, bf16[768,768]{1,0:T(8,128)(2,1)}, u32[]{:S(2)}) copy-start(bf16[768,768]{1,0:T(8,128)(2,1)} %param.36) | copy-start | bytes 3538948
  209.4 1.8 copy-start.54
  215.2 121.5 %reduce-scatter.3.cloned.1.call-start = ((), (), s32[]{:S(2)}) async-start(), calls=%async_computation.3 | async-start | bytes 3932160 | tf_op jit(solution)/shard_map/reduce_scatter | solution.py:133
  226.4 244.1 %all-reduce.12.cloned.1.call-start = ((), (), s32[]{:S(2)}) async-start(), calls=%async_computation.7 | async-start | bytes 9437184 | tf_op jit(solution)/shard_map/psum | solution.py:154
  226.5 7.2 %copy-start.25 = (bf16[2048,768]{1,0:T(8,128)(2,1)S(1)}, bf16[2048,768]{1,0:T(8,128)(2,1)}, u32[]{:S(2)}) copy-start(bf16[2048,768]{1,0:T(8,128)(2,1)} %copy-done.24) | copy-start | bytes 9437188
  226.5 7.1 %copy-start.43 = (bf16[2048,768]{1,0:T(8,128)(2,1)S(1)}, bf16[2048,768]{1,0:T(8,128)(2,1)}, u32[]{:S(2)}) copy-start(bf16[2048,768]{1,0:T(8,128)(2,1)} %all-gather.5.cloned.1.call-done) | copy-start | bytes 9437188
  237.8 98.9 %copy-start.42 = (f32[768]{0:T(1024)S(1)}, f32[768]{0:T(1024)}, u32[]{:S(2)}) copy-start(f32[768]{0:T(1024)} %param.39) | copy-start | bytes 9220
  237.8 391.7 %all-reduce.10.cloned.1.call-start = ((), (), s32[]{:S(2)}) async-start(), calls=%async_computation.6 | async-start | bytes 18874368 | tf_op jit(solution)/shard_map/psum | solution.py:192
  276.6 63.6 %copy-start.19 = (bf16[512,768]{1,0:T(8,128)(2,1)S(1)}, bf16[512,768]{1,0:T(8,128)(2,1)}, u32[]{:S(2)}) copy-start(bf16[512,768]{1,0:T(8,128)(2,1)} %param.21) | copy-start | bytes 2359300
  340.2 1.8 copy-start.46
  343.5 10.5 %copy-start.21 = (f32[12,64,512]{2,1,0:T(8,128)S(1)}, f32[12,64,512]{2,1,0:T(8,128)}, u32[]{:S(2)}) copy-start(f32[12,64,512]{2,1,0:T(8,128)} %get-tuple-element.71) | copy-start | bytes 4718596
  364.1 13.0 %copy-start.16 = (f32[512,12,32]{0,2,1:T(8,128)S(1)}, f32[512,12,32]{0,2,1:T(8,128)}, u32[]{:S(2)}) copy-start(f32[512,12,32]{0,2,1:T(8,128)} %copy-done.15) | copy-start | bytes 2359300
  364.1 13.0 %copy-start.18 = (f32[512,12,32]{0,2,1:T(8,128)S(1)}, f32[512,12,32]{0,2,1:T(8,128)}, u32[]{:S(2)}) copy-start(f32[512,12,32]{0,2,1:T(8,128)} %copy-done.17) | copy-start | bytes 2359300
  377.1 1.7 copy-start.12
  380.5 10.1 %slice-start = ((s8[12582912]{0:T(1024)(128)(4,1)}), s8[4194304]{0:T(1024)(128)(4,1)S(1)}, s32[]{:S(2)}) async-start(s8[12582912]{0:T(1024)(128)(4,1)} %bitcast.82), calls=%async_computation.8 | async-start | bytes 8388608
  381.2 1.8 copy-start.23
  381.2 9.4 %slice-start.1 = ((s8[12582912]{0:T(1024)(128)(4,1)}), s8[4194304]{0:T(1024)(128)(4,1)S(1)}, s32[]{:S(2)}) async-start(s8[12582912]{0:T(1024)(128)(4,1)} %bitcast.82), calls=%async_computation.9 | async-start | bytes 8388608
  381.4 3.8 copy-start.33
  383.0 5.1 copy-start.35
  385.1 5.4 slice-start.2
  405.2 15.0 %copy-start.34 = (bf16[512,12,64]{0,2,1:T(8,128)(2,1)S(1)}, bf16[512,12,64]{0,2,1:T(8,128)(2,1)}, u32[]{:S(2)}) copy-start(bf16[512,12,64]{0,2,1:T(8,128)(2,1)} %copy-done.33) | copy-start | bytes 2359300
  420.2 2.3 copy-start.36
  420.2 2.3 copy-start.48
  629.5 3.4 copy-start.30
  632.9 2.5 copy-start.29
  635.4 2.5 copy-start.28
  638.0 2.5 copy-start.27
  640.5 2.5 copy-start.26
  640.5 3.9 copy-start.1
  (16 other events, 20.3 us)
Sparse Core Ops, SparseCore 0:
  59.9 66.1 all-gather.2
  127.7 62.1 all-gather.4
  215.4 58.8 reduce-scatter.4
  276.4 60.2 reduce-scatter.2
  340.5 87.1 all-reduce.11
  436.6 192.8 all-reduce.9
where the time goes:
time: 661 us; the launch traced here: 651 us
  waiting for transfers between devices  378 us (57%)
  matrix products  144 us (22%)
  blocking collectives  57 us (9%)
  local copies, waits for them, and re-layouts  34.7 us (5%)
  other arithmetic  22.8 us (3%)
  between operations  15 us (2%)
    psum x1, waiting for transfers between devices, body(): lax.psum((gain_one_grad, bias_one_grad, query_weight_grad, wkey_grad, val...  159 us
    all_gather x1, waiting for transfers between devices, body(): gathered = lax.all_gather(second_low, 'tensor', axis=0, tiled=True)  65.5 us
    reduce_scatter x1, waiting for transfers between devices, body(): lax.psum_scatter(matmul(lax.slice_in_dim(hidden_low, 0, row_count * lax.a...  60.1 us
    all_gather x1, waiting for transfers between devices, body(): cot_gathered = lax.all_gather(cotangent, 'tensor', axis=0, tiled=True)  56.3 us
    psum x1, blocking collectives, body(): lax.psum((gain_one_grad, bias_one_grad, query_weight_grad, wkey_grad, val...  42.2 us
    reduce_scatter x1, waiting for transfers between devices, body(): lax.psum_scatter(right_product(inner_grad, w_up).astype(jnp.bfloat16), 't...  36 us
    dot_general x3, matrix products, attend(): jnp.einsum('otg,atg->toa', query_feature_map, key_feature_map, precision=...  34.1 us
    dot_general x3, matrix products, attend(): jnp.einsum('hqk,khd->qhd', weights, value_heads, precision=highest_precis...  32.3 us
  transfers between devices with their start and end apart: 6, of which 5 were waited for; matrix products, arithmetic and copies ran while one was open for 16% of the time, Pallas kernels for 0%

commit v1 on v0

--- a/solution.py
+++ b/solution.py
@@ -7,6 +7,24 @@
 
 HEADS = 12
 highest_precision = lax.Precision.HIGHEST
+
+
+def ring_gather(value, axis, dim):
+    ways, here, turn = (lax.axis_size(axis), lax.axis_index(axis), value.shape[dim])
+    dims = [n * ways if d == dim else n for d, n in enumerate(value.shape)]
+    full = lax.dynamic_update_slice_in_dim(
+        jnp.zeros(dims, value.dtype), value, here * turn, axis=dim
+    )
+    going_up = going_down = value
+    for far in range(1, ways // 2 + 1):
+        going_up = lax.ppermute(going_up, axis, [(d, (d + 1) % ways) for d in range(ways)])
+        full = lax.dynamic_update_slice_in_dim(full, going_up, (here - far) % ways * turn, axis=dim)
+        if 2 * far < ways:
+            going_down = lax.ppermute(going_down, axis, [(d, (d - 1) % ways) for d in range(ways)])
+            full = lax.dynamic_update_slice_in_dim(
+                full, going_down, (here + far) % ways * turn, axis=dim
+            )
+    return full
 
 
 def layer_norm(inputs, gain, shift):
@@ -139,7 +157,7 @@
         tiled=True,
     ).astype(jnp.float32)
     output = (middle + branch + b_down).astype(jnp.bfloat16)
-    cot_gathered = lax.all_gather(cotangent, "tensor", axis=0, tiled=True)
+    cot_gathered = ring_gather(cotangent, "tensor", 0)
     down_grad = left_product(hidden_low, cot_gathered)
     hidden_grad = right_product(cot_gathered, w_down)
     inner_grad = gelu_back(hidden_grad)[0].astype(jnp.bfloat16)

time: 661 us -> 646 us (0.977)
  waiting for transfers between devices: 378 us -> 329 us
  starting transfers between devices: 0.65 us -> 27.9 us
  local copies, waits for them, and re-layouts: 34.7 us -> 43.8 us
    ppermute x0 -> x3, waiting for transfers between devices: none -> 64.3 us  [the longest x2 43.2 us: ring_gather(): lax.ppermute(going_up, axis, [(d, (d + 1) % ways) for d in range(ways)])]
    all_gather x1, waiting for transfers between devices: 65.5 us -> 6.69 us  [body(): gathered = lax.all_gather(second_low, 'tensor', axis=0, tiled=True)]
    all_gather x1 -> x0, waiting for transfers between devices: 56.3 us -> none  [body(): cot_gathered = lax.all_gather(cotangent, 'tensor', axis=0, tiled=True)]
    ppermute x0 -> x3, starting transfers between devices: none -> 27.3 us  [the longest x2 25.2 us: ring_gather(): lax.ppermute(going_up, axis, [(d, (d + 1) % ways) for d in range(ways)])]
    dynamic_update_slice x0 -> x4, local copies, waits for them, and re-layouts: none -> 7.24 us  [the longest x2 4.18 us: ring_gather(): lax.dynamic_update_slice_in_dim(full, going_up, (here - far) % ways * tur...]
    unnamed x122 -> x126, local copies, waits for them, and re-layouts: 25.4 us -> 25.3 us
  transfers between devices with their start and end apart: 6 -> 8, of which waited for: 5 -> 7; matrix products, arithmetic and copies ran while one was open for 16% -> 16% of each run, Pallas kernels for 0% -> 0%
where the time goes in v1:
time: 646 us; the launch traced here: 636 us
  waiting for transfers between devices  329 us (51%)
  matrix products  141 us (22%)
  blocking collectives  57 us (9%)
  local copies, waits for them, and re-layouts  43.8 us (7%)
  starting transfers between devices  27.9 us (4%)
  other arithmetic  22.7 us (4%)
  between operations  15 us (2%)
    psum x1, waiting for transfers between devices, body(): lax.psum((gain_one_grad, bias_one_grad, query_weight_grad, wkey_grad, val...  159 us
    reduce_scatter x1, waiting for transfers between devices, body(): lax.psum_scatter(matmul(lax.slice_in_dim(hidden_low, 0, row_count * lax.a...  60.3 us
    ppermute x2, waiting for transfers between devices, ring_gather(): lax.ppermute(going_up, axis, [(d, (d + 1) % ways) for d in range(ways)])  43.2 us
    psum x1, blocking collectives, body(): lax.psum((gain_one_grad, bias_one_grad, query_weight_grad, wkey_grad, val...  42.2 us
    reduce_scatter x1, waiting for transfers between devices, body(): lax.psum_scatter(right_product(inner_grad, w_up).astype(jnp.bfloat16), 't...  38.7 us
    dot_general x3, matrix products, attend(): jnp.einsum('otg,atg->toa', query_feature_map, key_feature_map, precision=...  33.8 us
    dot_general x3, matrix products, attend(): jnp.einsum('hqk,khd->qhd', weights, value_heads, precision=highest_precis...  32.8 us
    dot_general x6, matrix products, right_product(): lax.dot_general(left, right, (((1,), (1,)), ((), ())), preferred_element_...  28.8 us
  transfers between devices with their start and end apart: 8, of which 7 were waited for; matrix products, arithmetic and copies ran while one was open for 16% of the time, Pallas kernels for 0%

profile of v1, /device:TPU:0, one launch (start us, length us, event | category | flops | bytes accessed | tf_op | source)
XLA Modules:
  0.0 636.5 jit_solution(9299695469706524760)
XLA Ops:
  9.8 2.1 convolution_add_fusion.1
  11.9 3.0 copy.50
  14.9 3.3 convolution_add_fusion
  18.3 3.0 copy.51
  21.6 2.3 multiply_subtract_fusion.1
  25.1 2.0 fusion.53
  27.1 2.0 fusion.59
  29.0 2.1 convolution_add_fusion.2
  31.1 3.0 copy.49
  34.1 12.3 %multiply_reduce_fusion = (f32[12,512]{1,0:T(8,128)S(1)}, f32[12,512,512]{1,2,0:T(8,128)S(1)}) fusion(f32[512,512]{0,1:T(8,128)S(1)} %compare_convert_fusion, f32[512,12,32]{0,2,1:T(8,128)} %fusion.59, f32[512,12,32]{0,2,1:T(8,128)} %fusion.53), kind=kOutput, calls=%fused_computation.5 | convolution fusion | flops 1214638080 | bytes 15228928 | tf_op jit(solution)/shard_map/jvp(otg,atg->toa)/dot_general | solution.py:76
  46.5 9.9 %fusion.37 = (bf16[512,12,64]{0,2,1:T(8,128)(2,1)S(1)}, f32[12,64,512]{2,1,0:T(8,128)}) fusion(f32[512,12]{0,1:T(8,128)S(1)} %bitcast.95, f32[512,12,64]{0,2,1:T(8,128)S(1)} %bitcast.84, f32[12,512,512]{1,2,0:T(8,128)S(1)} %get-tuple-element.69, f32[512,512]{0,1:T(8,128)S(1)} %compare_convert_fusion), kind=kOutput, calls=%fused_computation.67 | convolution fusion | flops 2419851264 | bytes 17588224 | tf_op jit(solution)/shard_map/jvp(hqk,khd->qhd)/dot_general | solution.py:82
  59.8 3.1 collective-permute-start
  62.8 2.1 collective-permute-start.1
  64.9 26.9 %collective-permute-done = bf16[512,768]{1,0:T(8,128)(2,1)} collective-permute-done((bf16[512,768]{1,0:T(8,128)(2,1)}, bf16[512,768]{1,0:T(8,128)(2,1)}, u32[]{:S(2)}, u32[]{:S(2)}) %collective-permute-start) | collective-permute-done | bytes 786464 | tf_op jit(solution)/shard_map/ppermute | solution.py:20
  91.9 22.1 %collective-permute-start.2 = (bf16[512,768]{1,0:T(8,128)(2,1)}, bf16[512,768]{1,0:T(8,128)(2,1)}, u32[]{:S(2)}, u32[]{:S(2)}) collective-permute-start(bf16[512,768]{1,0:T(8,128)(2,1)} %collective-permute-done), channel_id=1, source_target_pairs={{0,1},{1,2},{2,3},{3,0},{4,5},{5,6},{6,7},{7,4},{8,9},{9,10},{10,1... | collective-permute-start | bytes 2359304 | tf_op jit(solution)/shard_map/ppermute | solution.py:20
  114.0 2.0 broadcast_in_dim.14
  117.0 2.1 constant_dynamic-update-slice_fusion.2
  119.1 21.1 %collective-permute-done.1 = bf16[512,768]{1,0:T(8,128)(2,1)} collective-permute-done((bf16[512,768]{1,0:T(8,128)(2,1)}, bf16[512,768]{1,0:T(8,128)(2,1)}, u32[]{:S(2)}, u32[]{:S(2)}) %collective-permute-start.1) | collective-permute-done | bytes 786464 | tf_op jit(solution)/shard_map/ppermute | solution.py:23
  140.1 2.1 constant_dynamic-update-slice_fusion.1
  142.2 16.3 %collective-permute-done.2 = bf16[512,768]{1,0:T(8,128)(2,1)} collective-permute-done((bf16[512,768]{1,0:T(8,128)(2,1)}, bf16[512,768]{1,0:T(8,128)(2,1)}, u32[]{:S(2)}, u32[]{:S(2)}) %collective-permute-start.2) | collective-permute-done | bytes 786464 | tf_op jit(solution)/shard_map/ppermute | solution.py:20
  158.5 2.1 constant_dynamic-update-slice_fusion
  160.6 6.7 %all-gather.2.cloned.1.call-done = bf16[2048,768]{1,0:T(8,128)(2,1)} async-done(((bf16[512,768]{1,0:T(8,128)(2,1)}), bf16[2048,768]{1,0:T(8,128)(2,1)}) %all-gather.2.cloned.1.call-update) | async-done | bytes 3145744 | tf_op jit(solution)/shard_map/all_gather | solution.py:147
  167.3 4.9 fusion.109
  172.2 19.7 %convert_reduce_fusion = (f32[768]{0:T(1024)S(1)}, bf16[2048,768]{1,0:T(8,128)(2,1)S(1)}, f32[2048,768]{1,0:T(8,128)}) fusion(f32[2048,768]{1,0:T(8,128)S(1)} %fusion.109, f32[768]{0:T(1024)S(1)} %copy-done.42, bf16[2048,768]{1,0:T(8,128)(2,1)} %constant_dynamic-update-slice_fusion, bf16[768,768]{1,0:T(8,128)(2,1)S(1)} %copy-done), kind=kOutput, calls=%fused_computation.10 | convolution fusion | flops 2533883136 | bytes 20060160 | tf_op jit(solution)/shard_map/dot_general | solution.py:97
  193.5 4.0 convolution_convert_fusion
  197.8 5.5 multiply_convert_fusion
  204.9 4.0 convolution_convert_fusion.1
  209.0 7.1 %fusion.115 = f32[768,768]{1,0:T(8,128)} fusion(bf16[2048,768]{1,0:T(8,128)(2,1)} %copy-done.26, bf16[2048,768]{1,0:T(8,128)(2,1)} %constant_dynamic-update-slice_fusion), kind=kOutput, calls=%fused_computation.177 | convolution fusion | flops 2415919104 | bytes 8650752 | tf_op jit(solution)/shard_map/dot_general | solution.py:91
  216.1 4.2 fusion.114
  220.5 38.7 %reduce-scatter.5.cloned.1.call-done = bf16[512,768]{1,0:T(8,128)(2,1)} async-done(((bf16[2048,768]{1,0:T(8,128)(2,1)}), bf16[512,768]{1,0:T(8,128)(2,1)}) %reduce-scatter.5.cloned.1.call-update) | async-done | bytes 786448 | tf_op jit(solution)/shard_map/reduce_scatter | solution.py:166
  259.2 2.3 fusion.33
  261.5 60.3 %reduce-scatter.3.cloned.1.call-done = bf16[512,768]{1,0:T(8,128)(2,1)} async-done(((bf16[2048,768]{1,0:T(8,128)(2,1)}), bf16[512,768]{1,0:T(8,128)(2,1)}) %reduce-scatter.3.cloned.1.call-update) | async-done | bytes 786448 | tf_op jit(solution)/shard_map/reduce_scatter | solution.py:151
  321.8 3.5 fusion.105
  328.6 10.7 %fusion.35 = f32[12,512,512]{1,2,0:T(8,128)S(1)} fusion(f32[512,12,64]{0,2,1:T(8,128)S(1)} %bitcast.85, f32[512,12,64]{0,2,1:T(8,128)S(1)} %bitcast.86, f32[512,12]{0,1:T(8,128)S(1)} %bitcast.96), kind=kOutput, calls=%fused_computation.63 | convolution fusion | flops 2416312320 | bytes 15753216 | tf_op jit(solution)/shard_map/transpose(jvp(hqk,khd->qhd))/dot_general | solution.py:82
  340.8 8.6 %fusion.108 = (f32[512,12]{0,1:T(8,128)S(1)}, f32[512,12,32]{0,2,1:T(8,128)S(1)}) fusion(f32[512,12,32]{0,2,1:T(8,128)S(1)} %copy-done.9, f32[512,12,32]{0,2,1:T(8,128)S(1)} %copy-done.10, f32[12,512,512]{1,2,0:T(8,128)S(1)} %fusion.35, f32[12,512]{1,0:T(8,128)S(1)} %negate_bitcast_fusion, f32[512,512]{0,1:T(8,128)S(1)} %compare_convert_fusion), kind=kOutput, calls=%fused_computation.170 | convolution fusion | flops 1215031296 | bytes 16039936 | tf_op jit(solution)/shard_map/transpose(jvp(otg,atg->toa))/dot_general | solution.py:76
  349.4 12.9 %fusion.107 = (f32[512,12]{0,1:T(8,128)S(1)}, f32[512,12,32]{0,2,1:T(8,128)S(1)}) fusion(f32[512,12,32]{0,2,1:T(8,128)S(1)} %copy-done.10, f32[512,12,32]{0,2,1:T(8,128)S(1)} %copy-done.9, f32[12,512,512]{1,2,0:T(8,128)S(1)} %fusion.35, f32[12,512]{1,0:T(8,128)S(1)} %negate_bitcast_fusion, f32[512,512]{0,1:T(8,128)S(1)} %compare_convert_fusion), kind=kOutput, calls=%fused_computation.169 | convolution fusion | flops 1215031296 | bytes 16039936 | tf_op jit(solution)/shard_map/transpose(jvp(otg,atg->toa))/dot_general | solution.py:76
  362.4 1.7 fusion.40
  364.1 1.7 fusion.39
  368.3 2.2 fusion.113
  370.4 2.7 fusion.95
  373.2 2.5 fusion.97
  375.7 12.1 %convert_reduce_fusion.5 = (f32[12,64]{1,0:T(8,128)S(1)}, bf16[12,64,512]{2,1,0:T(8,128)(2,1)S(1)}) fusion(f32[12,512,512]{1,2,0:T(8,128)S(1)} %bitcast.83, f32[512,512]{0,1:T(8,128)S(1)} %compare_convert_fusion, f32[512,12,64]{0,2,1:T(8,128)S(1)} %bitcast.88, f32[512,12]{0,1:T(8,128)S(1)} %bitcast.97), kind=kOutput, calls=%fused_computation.74 | convolution fusion | flops 2420636928 | bytes 16018432 | tf_op jit(solution)/shard_map/transpose(jvp(hqk,khd->qhd))/dot_general | solution.py:82
  387.8 2.5 fusion.93
  390.3 14.8 %psum.125 = f32[768]{0:T(1024)} all-reduce(f32[768]{0:T(1024)S(1)} %get-tuple-element.40), channel_id=1, replica_groups=mesh['dp'=8,'tensor'=4] {'dp'}, use_global_device_ids=true, to_apply=%region_39.40 | all-reduce | flops 768 | bytes 6144 | tf_op jit(solution)/shard_map/psum | solution.py:172
  405.4 2.3 fusion.112
  413.5 42.2 %all-reduce.4 = (f32[768]{0:T(1024)}, f32[768]{0:T(1024)}, f32[768]{0:T(1024)}, f32[768]{0:T(1024)}, f32[768]{0:T(1024)}, /*index=5*/f32[768]{0:T(1024)}, f32[768]{0:T(1024)}, f32[768]{0:T(1024)}, f32[768]{0:T(1024)}) all-reduce(f32[768]{0:T(1024)S(1)} %get-tuple-element.18, ...), channel_id=1, replica_groups=mesh['dp'=8,'tensor'=4] {'dp','tensor'}, use_global_device_ids=true, to_apply=%region_18.19 | all-reduce | flops 6912 | bytes 55296 | tf_op jit(solution)/shard_map/psum | solution.py:210
  455.6 159.0 %all-reduce.10.cloned.1.call-done = (f32[768,768]{1,0:T(8,128)}, f32[768,768]{1,0:T(8,128)}, f32[768,768]{1,0:T(8,128)}, f32[768,768]{1,0:T(8,128)}) async-done(((f32[768,768]{1,0:T(8,128)}, f32[768,768]{1,0:T(8,128)}, f32[768,768]{1,0:T(8,128)}, f32[768,768]{1,0:T(8,128)}), (f32[768,768]{1,0:T(8,128)}, f32[768,768]{1,0:T(8,128)}, f32[768,768]{1,0:T(8,128)}, ...) | async-done | bytes 9437200 | tf_op jit(solution)/shard_map/psum | solution.py:210
  614.6 3.4 copy.74
  (176 shorter events, 36.7 us)
Async XLA Ops:
  7.2 165.0 %copy-start = (bf16[768,768]{1,0:T(8,128)(2,1)S(1)}, bf16[768,768]{1,0:T(8,128)(2,1)}, u32[]{:S(2)}) copy-start(bf16[768,768]{1,0:T(8,128)(2,1)} %param.38) | copy-start | bytes 3538948
  7.2 2.0 copy-start.4
  7.2 2.6 copy-start.39
  7.2 2.6 copy-start.54
  7.2 2.6 copy-start.50
  7.2 160.0 %all-gather.2.cloned.1.call-start = ((), (), s32[]{:S(2)}) async-start(), calls=%async_computation.2 | async-start | bytes 3932160 | tf_op jit(solution)/shard_map/all_gather | solution.py:147
  7.3 2.5 copy-start.48
  11.9 3.0 copy-start.51
  24.0 3.1 copy-start.11
  24.0 3.1 copy-start.13
  27.1 2.0 copy-start.32
  27.1 2.0 copy-start.52
  34.1 12.3 %copy-start.7 = (f32[512,768]{0,1:T(8,128)S(1)}, f32[512,768]{0,1:T(8,128)}, u32[]{:S(2)}) copy-start(f32[512,768]{0,1:T(8,128)} %copy.49) | copy-start | bytes 4718596
  46.4 9.9 %copy-start.2 = (f32[12,512,512]{1,2,0:T(8,128)}, f32[12,512,512]{1,2,0:T(8,128)S(1)}, u32[]{:S(2)}) copy-start(f32[12,512,512]{1,2,0:T(8,128)S(1)} %get-tuple-element.69) | copy-start | bytes 37748740
  46.5 9.9 %copy-start.46 = (bf16[768,768]{1,0:T(8,128)(2,1)S(1)}, bf16[768,768]{1,0:T(8,128)(2,1)}, u32[]{:S(2)}) copy-start(bf16[768,768]{1,0:T(8,128)(2,1)} %param.29) | copy-start | bytes 3538948
  46.5 9.9 %copy-start.53 = (f32[768]{0:T(1024)S(1)}, f32[768]{0:T(1024)}, u32[]{:S(2)}) copy-start(f32[768]{0:T(1024)} %param.33) | copy-start | bytes 9220
  59.7 199.5 %reduce-scatter.5.cloned.1.call-start = ((), (), s32[]{:S(2)}) async-start(), calls=%async_computation.4 | async-start | bytes 3932160 | tf_op jit(solution)/shard_map/reduce_scatter | solution.py:166
  59.8 32.1 %collective-permute-start = (bf16[512,768]{1,0:T(8,128)(2,1)}, bf16[512,768]{1,0:T(8,128)(2,1)}, u32[]{:S(2)}, u32[]{:S(2)}) collective-permute-start(bf16[512,768]{1,0:T(8,128)(2,1)} %param.21), channel_id=1, source_target_pairs={{0,1},{1,2},{2,3},{3,0},{4,5},{5,6},{6,7},{7,4},{8,9},{9,10},{10,1... | collective-permute-start | bytes 2359304 | tf_op jit(solution)/shard_map/ppermute | solution.py:20
  62.8 77.3 %collective-permute-start.1 = (bf16[512,768]{1,0:T(8,128)(2,1)}, bf16[512,768]{1,0:T(8,128)(2,1)}, u32[]{:S(2)}, u32[]{:S(2)}) collective-permute-start(bf16[512,768]{1,0:T(8,128)(2,1)} %param.21), channel_id=1, source_target_pairs={{0,3},{1,0},{2,1},{3,2},{4,7},{5,4},{6,5},{7,6},{8,11},{9,8},{10,9... | collective-permute-start | bytes 2359304 | tf_op jit(solution)/shard_map/ppermute | solution.py:23
  91.9 66.6 %collective-permute-start.2 = (bf16[512,768]{1,0:T(8,128)(2,1)}, bf16[512,768]{1,0:T(8,128)(2,1)}, u32[]{:S(2)}, u32[]{:S(2)}) collective-permute-start(bf16[512,768]{1,0:T(8,128)(2,1)} %collective-permute-done), channel_id=1, source_target_pairs={{0,1},{1,2},{2,3},{3,0},{4,5},{5,6},{6,7},{7,4},{8,9},{9,10},{10,1... | collective-permute-start | bytes 2359304 | tf_op jit(solution)/shard_map/ppermute | solution.py:20
  114.0 2.0 copy-start.19
  160.6 11.6 %copy-start.42 = (f32[768]{0:T(1024)S(1)}, f32[768]{0:T(1024)}, u32[]{:S(2)}) copy-start(f32[768]{0:T(1024)} %param.37) | copy-start | bytes 9220
  172.2 19.7 %copy-start.22 = (f32[2048,768]{1,0:T(8,128)}, f32[2048,768]{1,0:T(8,128)S(1)}, u32[]{:S(2)}) copy-start(f32[2048,768]{1,0:T(8,128)S(1)} %fusion.109) | copy-start | bytes 18874372
  172.2 21.3 %copy-start.45 = (bf16[768,768]{1,0:T(8,128)(2,1)S(1)}, bf16[768,768]{1,0:T(8,128)(2,1)}, u32[]{:S(2)}) copy-start(bf16[768,768]{1,0:T(8,128)(2,1)} %param.36) | copy-start | bytes 3538948
  197.6 124.3 %reduce-scatter.3.cloned.1.call-start = ((), (), s32[]{:S(2)}) async-start(), calls=%async_computation.3 | async-start | bytes 3932160 | tf_op jit(solution)/shard_map/reduce_scatter | solution.py:151
  208.9 246.7 %all-reduce.12.cloned.1.call-start = ((), (), s32[]{:S(2)}) async-start(), calls=%async_computation.6 | async-start | bytes 9437184 | tf_op jit(solution)/shard_map/psum | solution.py:172
  209.0 7.1 %copy-start.44 = (bf16[2048,768]{1,0:T(8,128)(2,1)S(1)}, bf16[2048,768]{1,0:T(8,128)(2,1)}, u32[]{:S(2)}) copy-start(bf16[2048,768]{1,0:T(8,128)(2,1)} %all-gather.2.cloned.1.call-done) | copy-start | bytes 9437188
  209.0 7.1 %copy-start.56 = (bf16[2048,768]{1,0:T(8,128)(2,1)S(1)}, bf16[2048,768]{1,0:T(8,128)(2,1)}, u32[]{:S(2)}) copy-start(bf16[2048,768]{1,0:T(8,128)(2,1)} %copy-done.55) | copy-start | bytes 9437188
  220.3 101.6 %copy-start.43 = (f32[768]{0:T(1024)S(1)}, f32[768]{0:T(1024)}, u32[]{:S(2)}) copy-start(f32[768]{0:T(1024)} %param.39) | copy-start | bytes 9220
  220.3 394.4 %all-reduce.10.cloned.1.call-start = ((), (), s32[]{:S(2)}) async-start(), calls=%async_computation.5 | async-start | bytes 18874368 | tf_op jit(solution)/shard_map/psum | solution.py:210
  261.5 63.8 %copy-start.20 = (bf16[512,768]{1,0:T(8,128)(2,1)S(1)}, bf16[512,768]{1,0:T(8,128)(2,1)}, u32[]{:S(2)}) copy-start(bf16[512,768]{1,0:T(8,128)(2,1)} %param.21) | copy-start | bytes 2359300
  328.6 10.7 %copy-start.23 = (f32[12,64,512]{2,1,0:T(8,128)S(1)}, f32[12,64,512]{2,1,0:T(8,128)}, u32[]{:S(2)}) copy-start(f32[12,64,512]{2,1,0:T(8,128)} %get-tuple-element.71) | copy-start | bytes 4718596
  349.4 12.9 %copy-start.16 = (f32[512,12,32]{0,2,1:T(8,128)S(1)}, f32[512,12,32]{0,2,1:T(8,128)}, u32[]{:S(2)}) copy-start(f32[512,12,32]{0,2,1:T(8,128)} %copy-done.15) | copy-start | bytes 2359300
  349.4 12.9 %copy-start.18 = (f32[512,12,32]{0,2,1:T(8,128)S(1)}, f32[512,12,32]{0,2,1:T(8,128)}, u32[]{:S(2)}) copy-start(f32[512,12,32]{0,2,1:T(8,128)} %copy-done.17) | copy-start | bytes 2359300
  365.8 9.9 %slice-start = ((s8[12582912]{0:T(1024)(128)(4,1)}), s8[4194304]{0:T(1024)(128)(4,1)S(1)}, s32[]{:S(2)}) async-start(s8[12582912]{0:T(1024)(128)(4,1)} %bitcast.82), calls=%async_computation.7 | async-start | bytes 8388608
  366.5 9.2 %slice-start.1 = ((s8[12582912]{0:T(1024)(128)(4,1)}), s8[4194304]{0:T(1024)(128)(4,1)S(1)}, s32[]{:S(2)}) async-start(s8[12582912]{0:T(1024)(128)(4,1)} %bitcast.82), calls=%async_computation.8 | async-start | bytes 8388608
  366.7 3.8 copy-start.34
  368.2 4.9 copy-start.36
  370.4 5.2 slice-start.2
  390.3 15.1 %copy-start.35 = (bf16[512,12,64]{0,2,1:T(8,128)(2,1)S(1)}, bf16[512,12,64]{0,2,1:T(8,128)(2,1)}, u32[]{:S(2)}) copy-start(bf16[512,12,64]{0,2,1:T(8,128)(2,1)} %copy-done.34) | copy-start | bytes 2359300
  405.4 2.3 copy-start.37
  405.4 2.3 copy-start.49
  614.6 3.4 copy-start.31
  618.0 2.5 copy-start.30
  620.5 2.5 copy-start.29
  623.0 2.5 copy-start.28
  625.6 2.5 copy-start.27
  625.6 3.9 copy-start.1
  (20 other events, 27.2 us)
Sparse Core Ops, SparseCore 0:
  59.8 107.3 all-gather.1
  197.7 61.4 reduce-scatter.4
  261.5 60.2 reduce-scatter.2
  325.6 87.1 all-reduce.11
  421.7 192.8 all-reduce.9
